TPU v7x, 256 devices: a whole 4x4x8 slice. The times are simulated.
256 devices in a mesh: block: 16 (over x, z_hi, core), day: 16 (over y, z_lo).
Axes of the slice: x: 4, y: 4, z: 8 (z_hi: 2, z_lo: 4; z = z_hi * 4 + z_lo), core: 2. Of those that a mesh axis runs over, the one named last changes fastest.
Arguments:
- spectra: bfloat16 [16, 8, 256, 2, 4096], P('day', None, 'block'), may hold values from -6 to 6
- hour_mask: int32 [16, 8, 256], P('day', None, 'block'), may hold values 0 or 1
- pairs: int32 [16, 2], replicated, may hold values from 0 to 15, as said below
Outputs:
- correlation: float32 [16, 256, 2048], P('block', 'day')
Inputs may be any that keep to these rules, and one draw needn't show every extreme that they name: `pairs`: rows k * 8 to (k + 1) * 8 - 1 form round k: every block appears in exactly one of its rows, so the two entries of a row differ.
All inputs are finite; a program needn't handle non-finite values. No bound on the sum of `hour_mask` on one device may be relied on, other than what follows from the above.
Results may differ from a plain program's by a relative error of at most 0.004.
Values may be sent and summed in bfloat16 or wider, within the bound.
No kernel may reach another device: no remote copies, remote signals or barrier semaphores. Data moves between devices by JAX's collectives and lax.ppermute only.
A program may use at most 128 MiB of HBM per device.

v0:
```python
import math
import jax
import jax.numpy as jnp
from jax import lax
from jax.sharding import PartitionSpec as P

F = 4096
LAGS = 2048


def tables(first, count, lags, width):
    bins = first + jnp.arange(count, dtype=jnp.int32)
    shifts = jnp.arange(lags, dtype=jnp.int32) - lags // 2
    turns = jnp.mod((bins + 1)[:, None] * shifts[None, :], 2 * width)
    phase = turns.astype(jnp.float32) * (math.pi / width)
    return (jnp.cos(phase), jnp.sin(phase))


def cross_terms(left, right):
    left_re = left[:, :, :, None, 0].astype(jnp.float32)
    left_im = left[:, :, :, None, 1].astype(jnp.float32)
    right_re = right[:, :, None, :, 0].astype(jnp.float32)
    right_im = right[:, :, None, :, 1].astype(jnp.float32)
    cross_re = jnp.sum(left_re * right_re + left_im * right_im, axis=0)
    cross_im = jnp.sum(left_im * right_re - left_re * right_im, axis=0)
    return (cross_re, cross_im)


def shards(spectra, hour_mask, pairs):
    blocks_count = lax.axis_size("block")
    days_count = lax.axis_size("day") * spectra.shape[0]
    stations = spectra.shape[2]
    values = spectra[0].astype(jnp.float32)
    power = jnp.mean(values[:, :, 0] * values[:, :, 0] + values[:, :, 1] * values[:, :, 1], axis=-1)
    factor = hour_mask[0].astype(jnp.float32) / jnp.sqrt(power + 1e-06)
    whitened = (values * factor[:, :, None, None]).astype(jnp.bfloat16)
    spread = lax.all_to_all(whitened, "block", split_axis=3, concat_axis=1, tiled=True)
    hours = spread.shape[0]
    band_part = spread.shape[3]
    grouped = spread.reshape(hours, blocks_count, stations, 2, band_part)
    left = jnp.take(grouped, pairs[:, 0], axis=1)
    right = jnp.take(grouped, pairs[:, 1], axis=1)
    cross_re, cross_im = cross_terms(left, right)
    pair_count = cross_re.shape[0]
    cross_re = cross_re.reshape(pair_count, stations * stations, band_part)
    cross_im = cross_im.reshape(pair_count, stations * stations, band_part)
    scale = 1.0 / math.sqrt(F * hours * days_count)
    high = lax.Precision.HIGHEST
    summed_re, summed_im = (
        lax.psum_scatter(cross_re, "day", scatter_dimension=1, tiled=True),
        lax.psum_scatter(cross_im, "day", scatter_dimension=1, tiled=True),
    )
    row_count = summed_re.shape[1]
    offset = lax.axis_index("block") * band_part
    cos_table, sin_table = tables(offset, band_part, LAGS, F)
    flat_re = summed_re.reshape(-1, band_part)
    flat_im = summed_im.reshape(-1, band_part)
    lagged = jnp.dot(flat_re, cos_table, precision=high) - jnp.dot(
        flat_im, sin_table, precision=high
    )
    result = lax.psum_scatter(lagged * scale, "block", scatter_dimension=0, tiled=True)
    return result.reshape(pair_count // blocks_count, row_count, LAGS)


def solution(mesh):
    in_specs = (P("day", None, "block", None, None), P("day", None, "block"), P())
    out_specs = P("block", "day", None)
    return jax.shard_map(shards, mesh=mesh, in_specs=in_specs, out_specs=out_specs, check_vma=False)
```

profile of v0, /device:TPU:8, one launch (start us, length us, event | category | flops | bytes accessed | tf_op | source)
XLA Modules:
  0.0 524.4 jit_solution(7528432776630027660)
XLA Ops:
  6.5 21.7 %copy.32 = bf16[1,8,16,2,4096]{2,1,3,4,0:T(8,128)(2,1)} copy(bf16[1,8,16,2,4096]{4,3,2,1,0:T(2,128)(2,1)} %param.5) | data formatting | bytes 4194304 | tf_op args[0]
  28.2 21.6 %bitcast_convert_fusion = f32[8,16,2,4096]{1,0,2,3:T(8,128)} fusion(bf16[1,8,16,2,4096]{2,1,3,4,0:T(8,128)(2,1)} %copy.32), kind=kLoop, calls=%fused_computation.9 | loop fusion | flops 1048576 | bytes 6291456 | tf_op jit(solution)/shard_map/convert_element_type | solution.py:33
  49.8 12.1 %fusion.1 = f32[8,16]{1,0:T(8,128)S(1)} fusion(f32[8,16,2,4096]{1,0,2,3:T(8,128)} %bitcast_convert_fusion), kind=kLoop, calls=%fused_computation.7 | loop fusion | flops 2097024 | bytes 4194816 | tf_op jit(solution)/shard_map/reduce_sum | solution.py:34
  62.0 7.6 %fusion.23 = bf16[4096,2,8,16]{3,2,1,0:T(8,128)(2,1)} fusion(f32[8,16]{1,0:T(8,128)S(1)} %bitcast_multiply_fusion, bf16[1,8,16,2,4096]{2,1,3,4,0:T(8,128)(2,1)S(1)} %bitcast.52), kind=kLoop, calls=%fused_computation.50 | loop fusion | flops 3145728 | bytes 4194816
  69.6 20.8 %reshape.98 = bf16[16,2,32768]{2,1,0:T(2,128)(2,1)} reshape(bf16[4096,2,8,16]{3,2,1,0:T(8,128)(2,1)} %fusion.23) | data formatting | bytes 4194304
  90.4 11.2 %all-to-all-start = ((bf16[16,2,32768]{2,1,0:T(2,128)(2,1)}), bf16[16,2,32768]{2,1,0:T(2,128)(2,1)S(1)}, u32[]{:S(2)}, u32[]{:S(2)}) async-start(bf16[16,2,32768]{2,1,0:T(2,128)(2,1)} %reshape.98), calls=%async_computation | async-start | bytes 4194304 | tf_op jit(solution)/shard_map/all_to_all | solution.py:37
  101.5 0.0 reduce-scatter.4.cloned.1.call-start
  101.6 53.3 %all-to-all-done = bf16[16,2,32768]{2,1,0:T(2,128)(2,1)S(1)} async-done(((bf16[16,2,32768]{2,1,0:T(2,128)(2,1)}), bf16[16,2,32768]{2,1,0:T(2,128)(2,1)S(1)}, u32[]{:S(2)}, u32[]{:S(2)}) %all-to-all-start) | async-done | bytes 2097184 | tf_op jit(solution)/shard_map/all_to_all | solution.py:37
  155.0 14.3 %reshape.99 = bf16[4096,2,8,16]{3,2,1,0:T(8,128)(2,1)} reshape(bf16[16,2,32768]{2,1,0:T(2,128)(2,1)S(1)} %all-to-all-done) | data formatting | bytes 4194304
  169.2 17.1 %copy.34 = bf16[8,16,2,16,256]{4,1,2,3,0:T(8,128)(2,1)S(1)} copy(bf16[8,16,2,16,256]{1,0,2,4,3:T(8,128)(2,1)} %bitcast.53) | data formatting | bytes 4194304 | tf_op jit(solution)/shard_map/all_to_all | solution.py:37
  186.3 2.0 gather_fusion
  188.3 2.0 gather_fusion.1
  190.3 2.6 select_bitcast_fusion
  193.0 0.6 fusion.12
  193.6 1.7 fusion.11
  195.4 23.3 %subtract_reduce_fusion = (f32[16,16,16,256]{3,2,1,0:T(8,128)}, f32[16,16,16,256]{3,2,1,0:T(8,128)}) fusion(f32[8,16,16,256]{3,2,0,1:T(8,128)S(1)} %get-tuple-element.12, f32[8,16,16,256]{3,2,0,1:T(8,128)S(1)} %get-tuple-element.14, f32[8,16,16,256]{3,2,0,1:T(8,128)S(1)} %get-tuple-element.13, f32[8,16,16,256]{3,2,0,1:T(8,128)} %get-tuple-element.15), kind=kLoop, calls=%fused_computation.2 | loop fusion | flops 65011712 | bytes 16777216 | tf_op jit(solution)/shard_map/reduce_sum | solution.py:25
  218.7 0.0 reduce-scatter.6.cloned.1.call-start
  218.8 0.7 reduce-scatter.6.cloned.1.call-update
  219.5 0.2 reduce-scatter.8.cloned.1.call-start
  219.7 95.2 %reduce-scatter.4.cloned.1.call-done = f32[16,16,256]{2,1,0:T(8,128)} async-done(((f32[16,256,256]{2,1,0:T(8,128)}), f32[16,16,256]{2,1,0:T(8,128)}) %reduce-scatter.4.cloned.1.call-update) | async-done | bytes 262160 | tf_op jit(solution)/shard_map/reduce_scatter | solution.py:50
  314.9 10.4 %fusion.7 = f32[256,2048]{1,0:T(8,128)S(1)} fusion(f32[256,256]{1,0:T(8,128)} %bitcast.58, s32[2048]{0:T(1024)S(1)} %iota_add_fusion, s32[256]{0:T(256)S(1)} %add_add_fusion), kind=kOutput, calls=%fused_computation.23 | convolution fusion | flops 1617952768 | bytes 2368512 | tf_op jit(solution)/shard_map/dot_general | solution.py:58
  325.3 92.5 %reduce-scatter.6.cloned.1.call-done = f32[16,16,256]{2,1,0:T(8,128)} async-done(((f32[16,256,256]{2,1,0:T(8,128)}), f32[16,16,256]{2,1,0:T(8,128)}) %reduce-scatter.6.cloned.1.call-update) | async-done | bytes 262160 | tf_op jit(solution)/shard_map/reduce_scatter | solution.py:51
  417.8 11.9 %fusion.2 = f32[256,2048]{1,0:T(8,128)} fusion(f32[256,2048]{1,0:T(8,128)S(1)} %fusion.7, f32[256,256]{1,0:T(8,128)} %bitcast.59, s32[2048]{0:T(1024)S(1)} %iota_add_fusion, s32[256]{0:T(256)S(1)} %add_add_fusion), kind=kOutput, calls=%fused_computation.16 | convolution fusion | flops 1619001344 | bytes 4465664 | tf_op jit(solution)/shard_map/dot_general | solution.py:58
  429.8 88.1 %reduce-scatter.8.cloned.1.call-done = f32[16,2048]{1,0:T(8,128)} async-done(((f32[256,2048]{1,0:T(8,128)}), f32[16,2048]{1,0:T(8,128)}) %reduce-scatter.8.cloned.1.call-update) | async-done | bytes 131088 | tf_op jit(solution)/shard_map/reduce_scatter | solution.py:61
  (21 shorter events, 0.1 us)
Async XLA Ops:
  28.2 33.7 %slice-start = ((s8[16777216]{0:T(1024)(128)(4,1)}), s8[4194304]{0:T(1024)(128)(4,1)S(1)}, s32[]{:S(2)}) async-start(s8[16777216]{0:T(1024)(128)(4,1)} %bitcast.51), calls=%async_computation.7 | async-start | bytes 8388608
  28.2 33.7 %slice-start.1 = ((s8[16777216]{0:T(1024)(128)(4,1)}), s8[4194304]{0:T(1024)(128)(4,1)S(1)}, s32[]{:S(2)}) async-start(s8[16777216]{0:T(1024)(128)(4,1)} %bitcast.51), calls=%async_computation.8 | async-start | bytes 8388608
  28.2 33.7 %slice-start.2 = ((s8[16777216]{0:T(1024)(128)(4,1)}), s8[4194304]{0:T(1024)(128)(4,1)S(1)}, s32[]{:S(2)}) async-start(s8[16777216]{0:T(1024)(128)(4,1)} %bitcast.51), calls=%async_computation.9 | async-start | bytes 8388608
  49.8 12.1 %copy-start = (s32[1,8,16]{2,1,0:T(8,128)S(1)}, s32[1,8,16]{2,1,0:T(8,128)}, u32[]{:S(2)}) copy-start(s32[1,8,16]{2,1,0:T(8,128)} %param.6) | copy-start | bytes 1540
  49.8 12.1 %slice-start.3 = ((s8[16777216]{0:T(1024)(128)(4,1)}), s8[4194304]{0:T(1024)(128)(4,1)S(1)}, s32[]{:S(2)}) async-start(s8[16777216]{0:T(1024)(128)(4,1)} %bitcast.51), calls=%async_computation.10 | async-start | bytes 8388608
  90.4 11.2 %copy-start.1 = (s32[16,2]{0,1:T(2,128)S(1)}, s32[16,2]{0,1:T(2,128)}, u32[]{:S(2)}) copy-start(s32[16,2]{0,1:T(2,128)} %param.7) | copy-start | bytes 388
  90.4 64.6 %all-to-all-start = ((bf16[16,2,32768]{2,1,0:T(2,128)(2,1)}), bf16[16,2,32768]{2,1,0:T(2,128)(2,1)S(1)}, u32[]{:S(2)}, u32[]{:S(2)}) async-start(bf16[16,2,32768]{2,1,0:T(2,128)(2,1)} %reshape.98), calls=%async_computation | async-start | bytes 4194304 | tf_op jit(solution)/shard_map/all_to_all | solution.py:37
  101.5 213.3 %reduce-scatter.4.cloned.1.call-start = ((), (), s32[]{:S(2)}) async-start(), calls=%async_computation.4 | async-start | bytes 4456448 | tf_op jit(solution)/shard_map/reduce_scatter | solution.py:50
  218.7 199.1 %reduce-scatter.6.cloned.1.call-start = ((), (), s32[]{:S(2)}) async-start(), calls=%async_computation.5 | async-start | bytes 4456448 | tf_op jit(solution)/shard_map/reduce_scatter | solution.py:51
  219.5 298.4 %reduce-scatter.8.cloned.1.call-start = ((), (), s32[]{:S(2)}) async-start(), calls=%async_computation.6 | async-start | bytes 2228224 | tf_op jit(solution)/shard_map/reduce_scatter | solution.py:61
Sparse Core Ops, SparseCore 0:
  218.8 95.9 reduce-scatter.3
  317.4 100.3 reduce-scatter.5
  429.9 87.8 reduce-scatter.7
where the time goes:
time: 525 us; the launch traced here: 524 us
  waiting for transfers between devices  330 us (63%)
  local copies, waits for them, and re-layouts  77.8 us (15%)
  other arithmetic  69.7 us (13%)
  matrix products  22.4 us (4%)
  between operations  13.3 us (3%)
  starting transfers between devices  11.5 us (2%)
    reduce_scatter x1, waiting for transfers between devices, shards(): lax.psum_scatter(cross_re, 'day', scatter_dimension=1, tiled=True)  95.2 us
    reduce_scatter x1, waiting for transfers between devices, shards(): lax.psum_scatter(cross_im, 'day', scatter_dimension=1, tiled=True)  92.5 us
    reduce_scatter x1, waiting for transfers between devices, shards(): lax.psum_scatter(lagged * scale, 'block', scatter_dimension=0, tiled=True)  88.1 us
    unnamed x15, local copies, waits for them, and re-layouts  56.7 us
    all_to_all x1, waiting for transfers between devices, shards(): lax.all_to_all(whitened, 'block', split_axis=3, concat_axis=1, tiled=True)  53.3 us
    reduce_sum x1, other arithmetic, cross_terms(): cross_im = jnp.sum(left_im * right_re - left_re * right_im, axis=0)  23.3 us
    convert_element_type x1, other arithmetic, shards(): values = spectra[0].astype(jnp.float32)  21.6 us
    all_to_all x1, local copies, waits for them, and re-layouts, shards(): lax.all_to_all(whitened, 'block', split_axis=3, concat_axis=1, tiled=True)  17.1 us
  transfers between devices with their start and end apart: 4, of which 4 were waited for; matrix products, arithmetic and copies ran while one was open for 2% of the time, Pallas kernels for 0%

commit v1 on v0

--- a/solution.py
+++ b/solution.py
@@ -34,7 +34,12 @@
     power = jnp.mean(values[:, :, 0] * values[:, :, 0] + values[:, :, 1] * values[:, :, 1], axis=-1)
     factor = hour_mask[0].astype(jnp.float32) / jnp.sqrt(power + 1e-06)
     whitened = (values * factor[:, :, None, None]).astype(jnp.bfloat16)
-    spread = lax.all_to_all(whitened, "block", split_axis=3, concat_axis=1, tiled=True)
+    spread = jnp.concatenate(
+        lax.all_to_all(
+            jnp.stack(jnp.split(whitened, lax.axis_size("block"), axis=3)), "block", 0, 0
+        ),
+        axis=1,
+    )
     hours = spread.shape[0]
     band_part = spread.shape[3]
     grouped = spread.reshape(hours, blocks_count, stations, 2, band_part)

time: 525 us -> 457 us (0.87); the launches traced: 524 us -> 450 us
  local copies, waits for them, and re-layouts: 77.8 us -> 29.1 us
  other arithmetic: 69.7 us -> 44 us
    unnamed x15 -> x21, local copies, waits for them, and re-layouts: 56.7 us -> 11.7 us
    convert_element_type x1, other arithmetic: 21.6 us -> 3.56 us  [shards(): values = spectra[0].astype(jnp.float32)]
    all_to_all x1 -> x0, local copies, waits for them, and re-layouts: 17.1 us -> none  [shards(): lax.all_to_all(whitened, 'block', split_axis=3, concat_axis=1, tiled=True)]
    unnamed x2 -> x0, other arithmetic: 7.61 us -> none
    reduce_sum x1, other arithmetic: 12.1 us -> 4.78 us  [shards(): jnp.mean(values[:, :, 0] * values[:, :, 0] + values[:, :, 1] * values[:,...]
    reduce_sum x1, other arithmetic: 23.3 us -> 16.2 us  [cross_terms(): cross_im = jnp.sum(left_im * right_re - left_re * right_im, axis=0)]
where the time goes in v1:
time: 457 us; the launch traced here: 450 us
  waiting for transfers between devices  329 us (72%)
  other arithmetic  44 us (10%)
  local copies, waits for them, and re-layouts  29.1 us (6%)
  matrix products  22.5 us (5%)
  between operations  13.5 us (3%)
  starting transfers between devices  11.7 us (3%)
    reduce_scatter x1, waiting for transfers between devices, shards(): lax.psum_scatter(cross_re, 'day', scatter_dimension=1, tiled=True)  95.3 us
    reduce_scatter x1, waiting for transfers between devices, shards(): lax.psum_scatter(cross_im, 'day', scatter_dimension=1, tiled=True)  92.5 us
    reduce_scatter x1, waiting for transfers between devices, shards(): lax.psum_scatter(lagged * scale, 'block', scatter_dimension=0, tiled=True)  88.1 us
    all_to_all x1, waiting for transfers between devices, shards(): lax.all_to_all(jnp.stack(jnp.split(whitened, lax.axis_size('block'), axis...  52.9 us
    reduce_sum x1, other arithmetic, cross_terms(): cross_im = jnp.sum(left_im * right_re - left_re * right_im, axis=0)  16.2 us
    dot_general x1, matrix products, shards(): jnp.dot(flat_im, sin_table, precision=high)  12.1 us
    unnamed x21, local copies, waits for them, and re-layouts  11.7 us
    all_to_all x1, starting transfers between devices, shards(): lax.all_to_all(jnp.stack(jnp.split(whitened, lax.axis_size('block'), axis...  11.2 us
  transfers between devices with their start and end apart: 4, of which 4 were waited for; matrix products, arithmetic and copies ran while one was open for 2% of the time, Pallas kernels for 0%

profile of v1, /device:TPU:8, one launch (start us, length us, event | category | flops | bytes accessed | tf_op | source)
XLA Modules:
  0.0 450.3 jit_solution(5404549512218910900)
XLA Ops:
  6.5 3.6 bitcast_convert_fusion
  10.1 4.8 %fusion.10 = f32[8,16]{1,0:T(8,128)S(1)} fusion(f32[8,16,2,4096]{3,2,1,0:T(2,128)S(1)} %bitcast_convert_fusion), kind=kLoop, calls=%fused_computation.34 | loop fusion | flops 2097024 | bytes 4194816 | tf_op jit(solution)/shard_map/reduce_sum | solution.py:34
  14.9 3.9 multiply_convert_fusion
  20.3 0.8 fusion.26
  24.2 0.8 fusion.21
  25.8 0.8 fusion.19
  26.6 0.8 fusion.18
  28.9 0.8 fusion.15
  31.2 11.2 %all-to-all-start = ((bf16[16,8,16,2,256]{4,3,2,1,0:T(2,128)(2,1)}), bf16[16,8,16,2,256]{4,3,2,1,0:T(2,128)(2,1)S(1)}, u32[]{:S(2)}, u32[]{:S(2)}) async-start(bf16[16,8,16,2,256]{4,3,2,1,0:T(2,128)(2,1)} %fusion.13), calls=%async_computation | async-start | bytes 4194304 | tf_op jit(solution)/shard_map/all_to_all | solution.py:38
  43.0 52.9 %all-to-all-done = bf16[16,8,16,2,256]{4,3,2,1,0:T(2,128)(2,1)S(1)} async-done(((bf16[16,8,16,2,256]{4,3,2,1,0:T(2,128)(2,1)}), bf16[16,8,16,2,256]{4,3,2,1,0:T(2,128)(2,1)S(1)}, u32[]{:S(2)}, u32[]{:S(2)}) %all-to-all-start) | async-done | bytes 2097184 | tf_op jit(solution)/shard_map/all_to_all | solution.py:38
  95.8 5.9 %gather_fusion = bf16[16,8,16,2,256]{4,3,2,1,0:T(2,128)(2,1)} fusion(bf16[8,16,16,2,256]{4,3,2,0,1:T(2,128)(2,1)S(1)} %bitcast.101, s32[1024]{0:T(1024)S(1)} %pad_clamp_fusion.1), kind=kCustom, calls=%fused_computation.clone | custom fusion | bytes 4194368 | tf_op jit(solution)/shard_map/jit(_take)/gather | solution.py:46
  101.7 5.9 %gather_fusion.1 = bf16[16,8,16,2,256]{4,3,2,1,0:T(2,128)(2,1)} fusion(bf16[8,16,16,2,256]{4,3,2,0,1:T(2,128)(2,1)S(1)} %bitcast.102, s32[1024]{0:T(1024)S(1)} %pad_clamp_fusion), kind=kCustom, calls=%fused_computation.1.clone | custom fusion | bytes 4194368 | tf_op jit(solution)/shard_map/jit(_take)/gather | solution.py:47
  107.6 5.9 %fusion.8 = (bf16[8,16,16,2,256]{4,3,2,0,1:T(2,128)(2,1)S(1)}, bf16[8,16,16,2,256]{4,3,2,0,1:T(2,128)(2,1)S(1)}) fusion(bf16[16,8,16,2,256]{4,3,2,1,0:T(2,128)(2,1)} %gather_fusion, pred[16]{0:T(512)(128)(4,1)S(1)} %get-tuple-element.8, bf16[16,8,16,2,256]{4,3,2,1,0:T(2,128)(2,1)} %gather_fusion.1, pred[16]{0:T(512)(128)(4,1)S(1)} %get-tuple-element.16), kind=kLoop, calls=%fused_computation.32 | loop fusion | flops 2097152 | bytes 8388640 | tf_op jit(solution)/shard_map/jit(_take)/select_n | solution.py:46
  113.5 4.8 %slice_convert_fusion.3 = (f32[8,16,16,1,256]{4,3,2,0,1:T(1,128)S(1)}, f32[8,16,16,1,256]{4,3,2,0,1:T(1,128)S(1)}) fusion(bf16[8,16,16,2,256]{4,3,2,0,1:T(2,128)(2,1)S(1)} %get-tuple-element.18), kind=kLoop, calls=%fused_computation.20 | loop fusion | flops 1048576 | bytes 6291456 | tf_op jit(solution)/shard_map/mul | solution.py:24
  118.6 4.8 %slice_convert_fusion.2 = (f32[8,16,16,1,256]{4,3,2,0,1:T(1,128)S(1)}, f32[8,16,16,1,256]{4,3,2,0,1:T(1,128)S(1)}) fusion(bf16[8,16,16,2,256]{4,3,2,0,1:T(2,128)(2,1)S(1)} %get-tuple-element.19), kind=kLoop, calls=%fused_computation.19 | loop fusion | flops 1048576 | bytes 6291456 | tf_op jit(solution)/shard_map/convert_element_type | solution.py:22
  123.3 1.6 copy.20
  125.0 1.5 copy.21
  126.5 1.6 copy.22
  128.0 16.2 %subtract_reduce_fusion = (f32[16,16,16,256]{3,2,1,0:T(8,128)}, f32[16,16,16,256]{3,2,1,0:T(8,128)}) fusion(f32[8,16,16,256]{3,2,1,0:T(8,128)} %bitcast.106, f32[8,16,16,256]{3,2,1,0:T(8,128)} %bitcast.107, f32[8,16,16,256]{3,2,1,0:T(8,128)} %bitcast.108, f32[8,16,16,256]{3,2,1,0:T(8,128)S(1)} %bitcast.105), kind=kLoop, calls=%fused_computation.2 | loop fusion | flops 65011712 | bytes 16777216 | tf_op jit(solution)/shard_map/reduce_sum | solution.py:25
  145.1 95.3 %reduce-scatter.4.cloned.1.call-done = f32[16,16,256]{2,1,0:T(8,128)} async-done(((f32[16,256,256]{2,1,0:T(8,128)}), f32[16,16,256]{2,1,0:T(8,128)}) %reduce-scatter.4.cloned.1.call-update) | async-done | bytes 262160 | tf_op jit(solution)/shard_map/reduce_scatter | solution.py:55
  240.4 10.4 %fusion.6 = f32[256,2048]{1,0:T(8,128)S(1)} fusion(f32[256,256]{1,0:T(8,128)} %bitcast.109, s32[2048]{0:T(1024)S(1)} %iota_add_fusion, s32[256]{0:T(256)S(1)} %add_add_fusion), kind=kOutput, calls=%fused_computation.30 | convolution fusion | flops 1617952768 | bytes 2368512 | tf_op jit(solution)/shard_map/dot_general | solution.py:63
  250.9 92.5 %reduce-scatter.6.cloned.1.call-done = f32[16,16,256]{2,1,0:T(8,128)} async-done(((f32[16,256,256]{2,1,0:T(8,128)}), f32[16,16,256]{2,1,0:T(8,128)}) %reduce-scatter.6.cloned.1.call-update) | async-done | bytes 262160 | tf_op jit(solution)/shard_map/reduce_scatter | solution.py:56
  343.4 12.1 %fusion = f32[256,2048]{1,0:T(8,128)} fusion(f32[256,2048]{1,0:T(8,128)S(1)} %fusion.6, f32[256,256]{1,0:T(8,128)} %bitcast.110, s32[2048]{0:T(1024)S(1)} %iota_add_fusion, s32[256]{0:T(256)S(1)} %add_add_fusion), kind=kOutput, calls=%fused_computation.13 | convolution fusion | flops 1619001344 | bytes 4465664 | tf_op jit(solution)/shard_map/dot_general | solution.py:63
  355.5 88.1 %reduce-scatter.8.cloned.1.call-done = f32[16,2048]{1,0:T(8,128)} async-done(((f32[256,2048]{1,0:T(8,128)}), f32[16,2048]{1,0:T(8,128)}) %reduce-scatter.8.cloned.1.call-update) | async-done | bytes 131088 | tf_op jit(solution)/shard_map/reduce_scatter | solution.py:66
  (30 shorter events, 10.1 us)
Async XLA Ops:
  10.1 4.8 %copy-start.1 = (s32[1,8,16]{2,1,0:T(8,128)S(1)}, s32[1,8,16]{2,1,0:T(8,128)}, u32[]{:S(2)}) copy-start(s32[1,8,16]{2,1,0:T(8,128)} %param.6) | copy-start | bytes 1540
  10.1 4.8 %copy-start = (bf16[1,8,16,2,4096]{4,3,2,1,0:T(2,128)(2,1)S(1)}, bf16[1,8,16,2,4096]{4,3,2,1,0:T(2,128)(2,1)}, u32[]{:S(2)}) copy-start(bf16[1,8,16,2,4096]{4,3,2,1,0:T(2,128)(2,1)} %param.5) | copy-start | bytes 6291460
  31.2 11.7 %copy-start.2 = (s32[16,2]{0,1:T(2,128)S(1)}, s32[16,2]{0,1:T(2,128)}, u32[]{:S(2)}) copy-start(s32[16,2]{0,1:T(2,128)} %param.7) | copy-start | bytes 388
  31.2 64.6 %all-to-all-start = ((bf16[16,8,16,2,256]{4,3,2,1,0:T(2,128)(2,1)}), bf16[16,8,16,2,256]{4,3,2,1,0:T(2,128)(2,1)S(1)}, u32[]{:S(2)}, u32[]{:S(2)}) async-start(bf16[16,8,16,2,256]{4,3,2,1,0:T(2,128)(2,1)} %fusion.13), calls=%async_computation | async-start | bytes 4194304 | tf_op jit(solution)/shard_map/all_to_all | solution.py:38
  42.4 198.0 %reduce-scatter.4.cloned.1.call-start = ((), (), s32[]{:S(2)}) async-start(), calls=%async_computation.4 | async-start | bytes 4456448 | tf_op jit(solution)/shard_map/reduce_scatter | solution.py:55
  144.3 199.1 %reduce-scatter.6.cloned.1.call-start = ((), (), s32[]{:S(2)}) async-start(), calls=%async_computation.5 | async-start | bytes 4456448 | tf_op jit(solution)/shard_map/reduce_scatter | solution.py:56
  145.0 298.5 %reduce-scatter.8.cloned.1.call-start = ((), (), s32[]{:S(2)}) async-start(), calls=%async_computation.6 | async-start | bytes 2228224 | tf_op jit(solution)/shard_map/reduce_scatter | solution.py:66
Sparse Core Ops, SparseCore 0:
  144.4 95.9 reduce-scatter.3
  243.0 100.3 reduce-scatter.5
  355.6 87.9 reduce-scatter.7
